TPU v7x, 512 devices: a whole 4x4x16 slice. The times are simulated.
512 devices in a mesh: grp: 16 (over z_lo, x), fsdp: 4 (over y), tp: 8 (over z_hi, core).
Axes of the slice: x: 4, y: 4, z: 16 (z_hi: 4, z_lo: 4; z = z_hi * 4 + z_lo), core: 2. Of those that a mesh axis runs over, the one named last changes fastest.
Arguments:
- frames: bfloat16 [3072, 5120], P('fsdp', 'grp'), may hold values from -6 to 6
- projector: bfloat16 [5120, 8192], P('grp', 'tp'), may hold values from -0.078125 to 0.078125
- text_token_embedding: bfloat16 [16384, 8192], P(('grp', 'fsdp'), 'tp'), may hold values from -6 to 6
- norm_gain_vector: float32 [8192], replicated, may hold values from 0.1 to 1.9
- frozen: bfloat16 [8192, 1024], P('fsdp', 'tp'), may hold values from -0.0625 to 0.0625
- adapter_down_map: bfloat16 [8192, 64], P('fsdp'), may hold values from -0.0625 to 0.0625
- adapter_up_map: bfloat16 [64, 1024], P(None, 'tp'), may hold values from -0.75 to 0.75
- clip_frame_length: int32 [4, 16, 16], P('fsdp'), may hold values from 1 to 6, as said below
- audio_first_token: int32 [4, 16, 16], P('fsdp'), may hold values from 0 to 255, as said below
- segment_document_index: int32 [16384], P(('grp', 'fsdp')), may hold values from 0 to 255, never falling along the last dimension, each value on 1 to 256 neighbouring positions
- keep_document_flags: int32 [256], replicated, may hold values 0 or 1
- cotangent: bfloat16 [16384, 1024], P(('grp', 'fsdp'), 'tp'), may hold values from -0.046875 to 0.046875
Outputs:
- value_output: bfloat16 [16384, 1024], P(('grp', 'fsdp'), 'tp')
- projector_grad: float32 [5120, 8192], P('grp', 'tp')
- down_map_gradient: float32 [8192, 64], P('tp')
- up_map_gradient: float32 [64, 1024], P(None, 'tp')
Inputs may be any that keep to these rules, and one draw needn't show every extreme that they name: `clip_frame_length`: entry [f, g, k] is the length of clip k of frame block f * 16 + g; the 16 clips of a block sum to 48, and one of them has exactly 6 frames. `audio_first_token`: entry [f, g, k] is the first token, among the 256 tokens of block k * 4 + f, of the audio slots of clip k of frame block f * 16 + g; the 16 clips that one token block takes lie in distinct aligned windows of 16 tokens.
All inputs are finite; a program needn't handle non-finite values.
Results may differ from a plain program's by a relative error of at most 0.018.
Values may be sent and summed in bfloat16 or wider, within the bound.
No kernel may reach another device: no remote copies, remote signals or barrier semaphores. Data moves between devices by JAX's collectives and lax.ppermute only.
A program may use at most 128 MiB of HBM per device.

v0:
```python
import jax
import jax.numpy as jnp
from jax import lax
from jax.sharding import PartitionSpec as P

adapter_scale = 2.0
norm_eps = 1e-05


def in_blocks(x, dim, length):
    shape = x.shape
    blocks = x.reshape(*shape[:dim], length, shape[dim] // length, *shape[dim + 1 :])
    return jnp.moveaxis(blocks, dim, 0)


def sent_and_summed(x, axis, dim):
    length = lax.axis_size(axis)
    blocks = lax.all_to_all(in_blocks(x, dim, length), axis, 0, 0, tiled=True)
    return jnp.sum(blocks.astype(jnp.float32), axis=0)


def side_by_side(arrays, axis, dim, along):
    ends, at = ([], 0)
    for a in arrays[:-1]:
        at += a.shape[along]
        ends.append(at)
    both = jnp.concatenate(arrays, axis=along)
    return tuple(jnp.split(lax.all_gather(both, axis, axis=dim, tiled=True), ends, axis=along))


def copy_for_each(x, axis):
    copies = jnp.broadcast_to(x, (lax.axis_size(axis), *x.shape))
    return lax.all_to_all(copies, axis, split_axis=0, concat_axis=0, tiled=True)


def over_copies(x, axis):
    return copy_for_each(x, axis).astype(jnp.float32).sum(axis=0)


def rows_for(lines, length):
    spare = -len(lines) % length
    return jnp.pad(lines, [(0, spare)] + [(0, 0)] * (lines.ndim - 1))


def in_order(blocks, dim):
    shape = list(blocks.shape[1:])
    shape[dim] *= blocks.shape[0]
    return jnp.moveaxis(blocks, 0, dim).reshape(shape)


def collect(x, axis, dim):
    return in_order(copy_for_each(x, axis), dim)


def sum_at_owner(x, axis, dim):
    blocks = in_blocks(x, dim, lax.axis_size(axis))
    arrived = lax.all_to_all(blocks, axis, split_axis=0, concat_axis=0, tiled=True)
    return arrived.sum(axis=0)


def total_of(x, axes):
    padded = rows_for(x, lax.axis_size(axes))
    whole = collect(sum_at_owner(padded, axes, 0), axes, 0)
    return lax.slice_in_dim(whole, 0, len(x)).reshape(x.shape)


def together(arrays, axis):
    flat, at, outs = (jnp.concatenate([a.reshape(-1) for a in arrays]), 0, [])
    so_far = total_of(flat, axis)
    for a in arrays:
        outs.append(so_far[at : at + a.size].reshape(a.shape))
        at += a.size
    return tuple(outs)


def pick_entry(grid_in, position, which_axis):
    matches = lax.broadcasted_iota(jnp.int32, grid_in.shape, which_axis) == position
    return jnp.sum(jnp.where(matches, grid_in, 0), axis=which_axis)


def contract_leading(left_side, right_side):
    return lax.dot_general(
        left_side, right_side, (((0,), (0,)), ((), ())), preferred_element_type=jnp.float32
    )


def contract_trailing(left_side, right_side):
    return lax.dot_general(
        left_side, right_side, (((1,), (1,)), ((), ())), preferred_element_type=jnp.float32
    )


def shards(
    frames,
    projector,
    text_token_embedding,
    norm_gain_vector,
    frozen,
    adapter_down_map,
    adapter_up_map,
    clip_frame_length,
    audio_first_token,
    segment_document_index,
    keep_document_flags,
    cotangent,
):
    grp_index = lax.axis_index("grp")
    tensor_shard_index = lax.axis_index("tp")
    tok_count, tensor_shard_width = text_token_embedding.shape
    group_count = clip_frame_length.shape[1]
    frame_count = frames.shape[0] // group_count
    slot_cap = 2 * frame_count // group_count
    slot_total = group_count * slot_cap
    full_width = tensor_shard_width * lax.axis_size("tp")
    own_sizes = pick_entry(clip_frame_length[0], grp_index, 0)
    own_starts = jnp.cumsum(own_sizes) - own_sizes
    slot_offset = lax.broadcasted_iota(jnp.int32, (group_count, slot_cap), 1)
    frame_slot = own_starts[:, None] + slot_offset
    slot_live = slot_offset < own_sizes[:, None]
    frame_iota = lax.broadcasted_iota(jnp.int32, (group_count, slot_cap, frame_count), 2)
    sender = (
        ((frame_iota == frame_slot[:, :, None]) & slot_live[:, :, None])
        .astype(jnp.bfloat16)
        .reshape(slot_total, frame_count)
    )
    in_sizes = pick_entry(clip_frame_length[0], grp_index, 1)
    arrive_at = pick_entry(audio_first_token[0], grp_index, 1)
    token_iota = lax.broadcasted_iota(jnp.int32, (tok_count, group_count, slot_cap), 0)
    receive_mask = (token_iota == (arrive_at[:, None] + slot_offset)[None]) & (
        slot_offset < in_sizes[:, None]
    )[None]
    receiving_device = receive_mask.astype(jnp.bfloat16).reshape(tok_count, slot_total)
    is_audio = jnp.any(receive_mask, axis=(1, 2))
    embedded = sent_and_summed(
        jnp.dot(frames, projector, preferred_element_type=jnp.float32).astype(jnp.bfloat16),
        "grp",
        0,
    ).astype(jnp.bfloat16)
    outgoing = (
        jnp.dot(sender, embedded, preferred_element_type=jnp.float32)
        .astype(jnp.bfloat16)
        .reshape(group_count, slot_cap, tensor_shard_width)
    )
    incoming = lax.all_to_all(outgoing, "grp", split_axis=0, concat_axis=0, tiled=True).reshape(
        slot_total, tensor_shard_width
    )
    audio_part = jnp.dot(receiving_device, incoming, preferred_element_type=jnp.float32).astype(
        jnp.bfloat16
    )
    inputs = jnp.where(is_audio[:, None], audio_part, text_token_embedding)
    gathered = lax.all_gather(inputs, "tp", axis=1, tiled=True)
    widened = gathered.astype(jnp.float32)
    mean_sq = jnp.mean(widened * widened, axis=1)
    inv_rms = lax.rsqrt(mean_sq + norm_eps)
    normalized_input = (widened * inv_rms[:, None] * norm_gain_vector[None, :]).astype(jnp.bfloat16)
    frozen_complete, adapter_complete = side_by_side((frozen, adapter_down_map), "fsdp", 0, 1)
    base_output = jnp.dot(normalized_input, frozen_complete, preferred_element_type=jnp.float32)
    lower_rank_rows = jnp.dot(
        normalized_input, adapter_complete, preferred_element_type=jnp.float32
    )
    lower_halfway = lower_rank_rows.astype(jnp.bfloat16)
    value_output = (
        base_output
        + adapter_scale * jnp.dot(lower_halfway, adapter_up_map, preferred_element_type=jnp.float32)
    ).astype(jnp.bfloat16)
    doc_iota = lax.broadcasted_iota(jnp.int32, (tok_count, keep_document_flags.shape[0]), 1)
    weight_tok = jnp.sum(
        jnp.where(segment_document_index[:, None] == doc_iota, keep_document_flags[None, :], 0),
        axis=1,
    )
    output_gradient = cotangent * weight_tok.astype(jnp.bfloat16)[:, None]
    adapter_portion = adapter_scale * contract_trailing(output_gradient, adapter_up_map)
    dot_portion = jnp.sum(output_gradient.astype(jnp.float32) * base_output, axis=1) + jnp.sum(
        adapter_portion * lower_rank_rows, axis=1
    )
    adapter_gradient, row_dot_products = (
        over_copies(adapter_portion.astype(jnp.bfloat16), "tp").astype(jnp.float32),
        over_copies(dot_portion.astype(jnp.bfloat16), "tp").astype(jnp.float32),
    )
    adapter_halfway = adapter_gradient.astype(jnp.bfloat16)
    up_portion = adapter_scale * contract_leading(lower_halfway, output_gradient)
    local_normalized = lax.dynamic_slice_in_dim(
        normalized_input, tensor_shard_index * tensor_shard_width, tensor_shard_width, 1
    )
    down_portion = contract_leading(local_normalized, adapter_halfway)
    down_map_gradient, up_map_gradient = together((down_portion, up_portion), ("grp", "fsdp"))
    slot_grad = contract_leading(receiving_device, output_gradient).astype(jnp.bfloat16)
    slot_adapter = contract_leading(receiving_device, adapter_halfway).astype(jnp.bfloat16)
    slot_stats = lax.dot_general(
        receiving_device.astype(jnp.float32),
        jnp.stack([inv_rms, row_dot_products], axis=1),
        (((0,), (0,)), ((), ())),
        precision=lax.Precision.HIGHEST,
        preferred_element_type=jnp.float32,
    )
    spread_rows = contract_trailing(slot_grad, frozen_complete)
    reduced_result = lax.psum_scatter(
        spread_rows.astype(jnp.bfloat16), "tp", scatter_dimension=1, tiled=True
    ).astype(jnp.float32)
    local_adapter = lax.dynamic_slice_in_dim(
        adapter_complete, tensor_shard_index * tensor_shard_width, tensor_shard_width, 0
    )
    gradient_norm = reduced_result + contract_trailing(slot_adapter, local_adapter)
    own_gain = lax.dynamic_slice_in_dim(
        norm_gain_vector, tensor_shard_index * tensor_shard_width, tensor_shard_width, 0
    )
    slot_inv = slot_stats[:, 0:1]
    slot_dot = slot_stats[:, 1:2]
    grad_rows = (
        slot_inv * own_gain[None, :] * gradient_norm
        - incoming.astype(jnp.float32) * (slot_inv * slot_inv * slot_dot / full_width)
    ).astype(jnp.bfloat16)
    returned = lax.all_to_all(
        grad_rows.reshape(group_count, slot_cap, tensor_shard_width),
        "grp",
        split_axis=0,
        concat_axis=0,
        tiled=True,
    ).reshape(slot_total, tensor_shard_width)
    frame_grad = contract_leading(sender, returned).astype(jnp.bfloat16)
    proj_part = contract_leading(frames, collect(frame_grad, "grp", 0))
    projector_grad = over_copies(proj_part.astype(jnp.bfloat16), "fsdp").astype(jnp.float32)
    return (value_output, projector_grad, down_map_gradient, up_map_gradient)


def solution(mesh):
    in_specs = (
        P("fsdp", "grp"),
        P("grp", "tp"),
        P(("grp", "fsdp"), "tp"),
        P(),
        P("fsdp", "tp"),
        P("fsdp", None),
        P(None, "tp"),
        P("fsdp", None, None),
        P("fsdp", None, None),
        P(("grp", "fsdp")),
        P(),
        P(("grp", "fsdp"), "tp"),
    )
    out_specs = (P(("grp", "fsdp"), "tp"), P("grp", "tp"), P("tp", None), P(None, "tp"))
    return jax.shard_map(shards, mesh=mesh, in_specs=in_specs, out_specs=out_specs, check_vma=False)
```

profile of v0, /device:TPU:64, one launch (start us, length us, event | category | flops | bytes accessed | tf_op | source)
XLA Modules:
  0.0 395.2 jit_solution(4861010309446714678)
XLA Ops:
  7.2 1.1 copy-done
  8.3 3.2 convolution_convert_fusion.1
  11.5 8.7 %all-to-all-start = ((bf16[16,48,1024]{2,1,0:T(8,128)(2,1)}), bf16[16,48,1024]{2,1,0:T(8,128)(2,1)S(1)}, u32[]{:S(2)}, u32[]{:S(2)}) async-start(bf16[16,48,1024]{2,1,0:T(8,128)(2,1)} %bitcast.51), calls=%async_computation | async-start | bytes 3145728 | tf_op jit(solution)/shard_map/all_to_all | solution.py:18
  20.5 1.2 pad_maximum_fusion
  23.2 33.4 %all-to-all-done = bf16[16,48,1024]{2,1,0:T(8,128)(2,1)S(1)} async-done(((bf16[16,48,1024]{2,1,0:T(8,128)(2,1)}), bf16[16,48,1024]{2,1,0:T(8,128)(2,1)S(1)}, u32[]{:S(2)}, u32[]{:S(2)}) %all-to-all-start) | async-done | bytes 1572896 | tf_op jit(solution)/shard_map/all_to_all | solution.py:18
  57.2 0.8 reshape.193
  58.0 5.1 %all-to-all-start.1 = ((bf16[16,6,1024]{2,1,0:T(8,128)(2,1)}), bf16[16,6,1024]{2,1,0:T(8,128)(2,1)S(1)}, u32[]{:S(2)}, u32[]{:S(2)}) async-start(bf16[16,6,1024]{2,1,0:T(8,128)(2,1)} %reshape.193), calls=%async_computation.1 | async-start | bytes 524288 | tf_op jit(solution)/shard_map/all_to_all | solution.py:144
  63.3 7.9 %all-to-all-done.1 = bf16[16,6,1024]{2,1,0:T(8,128)(2,1)S(1)} async-done(((bf16[16,6,1024]{2,1,0:T(8,128)(2,1)}), bf16[16,6,1024]{2,1,0:T(8,128)(2,1)S(1)}, u32[]{:S(2)}, u32[]{:S(2)}) %all-to-all-start.1) | async-done | bytes 196640 | tf_op jit(solution)/shard_map/all_to_all | solution.py:144
  71.2 2.3 fusion.8
  73.8 7.2 %all-gather.5.cloned.1.call-done = bf16[8192,192]{1,0:T(8,128)(2,1)} async-done(((bf16[2048,192]{1,0:T(8,128)(2,1)}), bf16[8192,192]{1,0:T(8,128)(2,1)}) %all-gather.5.cloned.1.call-update) | async-done | bytes 3145744 | tf_op jit(solution)/shard_map/all_gather | solution.py:28
  81.1 3.8 convolution_convert_fusion
  84.9 92.6 %all-gather.3.cloned.1.call-done = bf16[256,8192]{1,0:T(8,128)(2,1)} async-done(((bf16[256,1024]{1,0:T(8,128)(2,1)}), bf16[256,8192]{1,0:T(8,128)(2,1)}) %all-gather.3.cloned.1.call-update) | async-done | bytes 4194320 | tf_op jit(solution)/shard_map/all_gather | solution.py:151
  177.5 3.3 fusion
  180.9 1.2 fusion.2
  182.1 1.0 copy-done.2
  183.1 1.4 fusion.71
  185.1 1.5 multiply_reduce_fusion
  187.9 16.1 %all_to_all.51 = bf16[8,2,128]{2,1,0:T(2,128)(2,1)S(1)} all-to-all(bf16[8,2,128]{2,1,0:T(2,128)(2,1)S(1)} %reshape.203), channel_id=1, replica_groups=mesh['grp'=16,'fsdp'=4,'tp'=8] {'tp'}, dimensions={0} | all-to-all | bytes 8192 | tf_op jit(solution)/shard_map/all_to_all | solution.py:33
  204.6 4.0 %all-to-all-start.3 = ((bf16[8,256,64]{1,2,0:T(8,128)(2,1)}), bf16[8,256,64]{1,2,0:T(8,128)(2,1)}, u32[]{:S(2)}, u32[]{:S(2)}) async-start(bf16[8,256,64]{1,2,0:T(8,128)(2,1)} %broadcast_in_dim.61), calls=%async_computation.4 | async-start | bytes 524288 | tf_op jit(solution)/shard_map/all_to_all | solution.py:33
  209.3 0.8 reshape.198
  211.0 18.4 %all-to-all-done.3 = bf16[8,256,64]{1,2,0:T(8,128)(2,1)} async-done(((bf16[8,256,64]{1,2,0:T(8,128)(2,1)}), bf16[8,256,64]{1,2,0:T(8,128)(2,1)}, u32[]{:S(2)}, u32[]{:S(2)}) %all-to-all-start.3) | async-done | bytes 262176 | tf_op jit(solution)/shard_map/all_to_all | solution.py:33
  229.4 1.0 reduce_sum.123
  230.4 1.4 fusion.16
  231.8 0.8 reshape.196
  232.6 15.0 %reduce-scatter.2.cloned.1.call-done = bf16[96,1024]{1,0:T(8,128)(2,1)} async-done(((bf16[96,8192]{1,0:T(8,128)(2,1)}), bf16[96,1024]{1,0:T(8,128)(2,1)}) %reduce-scatter.2.cloned.1.call-update) | async-done | bytes 196624 | tf_op jit(solution)/shard_map/reduce_scatter | solution.py:197
  247.7 1.5 fusion.11
  249.2 0.8 reshape.194
  250.0 7.0 %all-to-all-start.4 = ((bf16[16,6,1024]{2,1,0:T(8,128)(2,1)}), bf16[16,6,1024]{2,1,0:T(8,128)(2,1)S(1)}, u32[]{:S(2)}, u32[]{:S(2)}) async-start(bf16[16,6,1024]{2,1,0:T(8,128)(2,1)} %reshape.194), calls=%async_computation.5 | async-start | bytes 524288 | tf_op jit(solution)/shard_map/all_to_all | solution.py:213
  257.0 1.7 pad_maximum_fusion.1
  258.7 6.0 %all-to-all-done.4 = bf16[16,6,1024]{2,1,0:T(8,128)(2,1)S(1)} async-done(((bf16[16,6,1024]{2,1,0:T(8,128)(2,1)}), bf16[16,6,1024]{2,1,0:T(8,128)(2,1)S(1)}, u32[]{:S(2)}, u32[]{:S(2)}) %all-to-all-start.4) | async-done | bytes 196640 | tf_op jit(solution)/shard_map/all_to_all | solution.py:213
  264.6 12.8 %all-to-all-start.7 = ((f32[64,1,1152]{2,1,0:T(1,128)}), f32[64,1,1152]{2,1,0:T(1,128)S(1)}, u32[]{:S(2)}, u32[]{:S(2)}) async-start(f32[64,1,1152]{2,1,0:T(1,128)} %bitcast.13), calls=%async_computation.8 | async-start | bytes 589824 | tf_op jit(solution)/shard_map/all_to_all | solution.py:57
  278.0 11.3 %all-to-all-done.7 = f32[64,1,1152]{2,1,0:T(1,128)S(1)} async-done(((f32[64,1,1152]{2,1,0:T(1,128)}), f32[64,1,1152]{2,1,0:T(1,128)S(1)}, u32[]{:S(2)}, u32[]{:S(2)}) %all-to-all-start.7) | async-done | bytes 294944 | tf_op jit(solution)/shard_map/all_to_all | solution.py:57
  289.4 1.3 broadcast_in_dim.62
  290.7 5.7 %all-to-all-start.5 = ((bf16[16,48,1024]{2,1,0:T(8,128)(2,1)}), bf16[16,48,1024]{2,1,0:T(8,128)(2,1)S(1)}, u32[]{:S(2)}, u32[]{:S(2)}) async-start(bf16[16,48,1024]{2,1,0:T(8,128)(2,1)} %broadcast_in_dim.62), calls=%async_computation.6 | async-start | bytes 3145728 | tf_op jit(solution)/shard_map/all_to_all | solution.py:33
  296.6 35.8 %all-to-all-done.5 = bf16[16,48,1024]{2,1,0:T(8,128)(2,1)S(1)} async-done(((bf16[16,48,1024]{2,1,0:T(8,128)(2,1)}), bf16[16,48,1024]{2,1,0:T(8,128)(2,1)S(1)}, u32[]{:S(2)}, u32[]{:S(2)}) %all-to-all-start.5) | async-done | bytes 1572896 | tf_op jit(solution)/shard_map/all_to_all | solution.py:33
  332.4 0.9 broadcast_in_dim.64
  333.2 6.7 %all-to-all-start.8 = ((f32[64,1,1152]{2,1,0:T(1,128)}), f32[64,1,1152]{2,1,0:T(1,128)S(1)}, u32[]{:S(2)}, u32[]{:S(2)}) async-start(f32[64,1,1152]{2,1,0:T(1,128)} %broadcast_in_dim.64), calls=%async_computation.9 | async-start | bytes 589824 | tf_op jit(solution)/shard_map/all_to_all | solution.py:33
  339.9 1.7 fusion.7
  341.6 8.8 %all-to-all-done.8 = f32[64,1,1152]{2,1,0:T(1,128)S(1)} async-done(((f32[64,1,1152]{2,1,0:T(1,128)}), f32[64,1,1152]{2,1,0:T(1,128)S(1)}, u32[]{:S(2)}, u32[]{:S(2)}) %all-to-all-start.8) | async-done | bytes 294944 | tf_op jit(solution)/shard_map/all_to_all | solution.py:33
  350.5 1.8 broadcast_in_dim.63
  352.3 3.7 all-to-all-start.6
  356.9 2.4 reduce.5
  359.3 1.9 slice.20
  361.2 1.9 slice.24
  363.1 1.9 copy.97
  365.0 1.4 slice.25
  366.4 20.7 %all-to-all-done.6 = bf16[4,320,1024]{2,1,0:T(8,128)(2,1)S(1)} async-done(((bf16[4,320,1024]{2,1,0:T(8,128)(2,1)}), bf16[4,320,1024]{2,1,0:T(8,128)(2,1)S(1)}, u32[]{:S(2)}, u32[]{:S(2)}) %all-to-all-start.6) | async-done | bytes 2621472 | tf_op jit(solution)/shard_map/all_to_all | solution.py:33
  387.2 1.5 convert_reduce_fusion
  (95 shorter events, 8.8 us)
Async XLA Ops:
  7.2 1.1 copy-start
  7.2 13.0 %copy-start.6 = (bf16[2048,64]{0,1:T(8,128)(2,1)S(1)}, bf16[2048,64]{0,1:T(8,128)(2,1)}, u32[]{:S(2)}) copy-start(bf16[2048,64]{0,1:T(8,128)(2,1)} %param.17) | copy-start | bytes 786436
  7.2 13.3 %copy-start.5 = (bf16[2048,128]{1,0:T(8,128)(2,1)S(1)}, bf16[2048,128]{1,0:T(8,128)(2,1)}, u32[]{:S(2)}) copy-start(bf16[2048,128]{1,0:T(8,128)(2,1)} %param.16) | copy-start | bytes 1572868
  11.5 10.3 %copy-start.12 = (s32[1,16,16]{2,1,0:T(8,128)S(1)}, s32[1,16,16]{2,1,0:T(8,128)}, u32[]{:S(2)}) copy-start(s32[1,16,16]{2,1,0:T(8,128)} %param.19) | copy-start | bytes 3076
  11.5 10.3 %copy-start.13 = (s32[1,16,16]{2,1,0:T(8,128)S(1)}, s32[1,16,16]{2,1,0:T(8,128)}, u32[]{:S(2)}) copy-start(s32[1,16,16]{2,1,0:T(8,128)} %param.20) | copy-start | bytes 3076
  11.5 45.2 %all-to-all-start = ((bf16[16,48,1024]{2,1,0:T(8,128)(2,1)}), bf16[16,48,1024]{2,1,0:T(8,128)(2,1)S(1)}, u32[]{:S(2)}, u32[]{:S(2)}) async-start(bf16[16,48,1024]{2,1,0:T(8,128)(2,1)} %bitcast.51), calls=%async_computation | async-start | bytes 3145728 | tf_op jit(solution)/shard_map/all_to_all | solution.py:18
  20.2 60.9 %all-gather.5.cloned.1.call-start = ((), (), s32[]{:S(2)}) async-start(), calls=%async_computation.11 | async-start | bytes 5242880 | tf_op jit(solution)/shard_map/all_gather | solution.py:28
  21.7 51.8 %copy-start.7 = (bf16[256,128]{1,0:T(8,128)(2,1)S(1)}, bf16[256,128]{1,0:T(8,128)(2,1)}, u32[]{:S(2)}) copy-start(bf16[256,128]{1,0:T(8,128)(2,1)} %param.23) | copy-start | bytes 196612
  21.7 51.9 %copy-start.18 = (s32[256]{0:T(256)S(1)}, s32[256]{0:T(256)}, u32[]{:S(2)}) copy-start(s32[256]{0:T(256)} %param.22) | copy-start | bytes 3076
  21.7 51.9 %copy-start.19 = (s32[256]{0:T(256)S(1)}, s32[256]{0:T(256)}, u32[]{:S(2)}) copy-start(s32[256]{0:T(256)} %param.21) | copy-start | bytes 3076
  21.9 1.3 copy-start.10
  22.2 0.5 copy-start.16
  23.2 187.1 %copy-start.14 = (s32[96]{0:T(128)}, s32[96]{0:T(128)S(1)}, u32[]{:S(2)}) copy-start(s32[96]{0:T(128)S(1)} %get-tuple-element.41) | copy-start | bytes 1156
  23.2 187.1 %copy-start.15 = (pred[96]{0:T(512)(128)(4,1)}, pred[96]{0:T(512)(128)(4,1)S(1)}, u32[]{:S(2)}) copy-start(pred[96]{0:T(512)(128)(4,1)S(1)} %get-tuple-element.39) | copy-start | bytes 292
  58.0 13.2 %all-to-all-start.1 = ((bf16[16,6,1024]{2,1,0:T(8,128)(2,1)}), bf16[16,6,1024]{2,1,0:T(8,128)(2,1)S(1)}, u32[]{:S(2)}, u32[]{:S(2)}) async-start(bf16[16,6,1024]{2,1,0:T(8,128)(2,1)} %reshape.193), calls=%async_computation.1 | async-start | bytes 524288 | tf_op jit(solution)/shard_map/all_to_all | solution.py:144
  63.1 114.4 %all-gather.3.cloned.1.call-start = ((), (), s32[]{:S(2)}) async-start(), calls=%async_computation.10 | async-start | bytes 4718592 | tf_op jit(solution)/shard_map/all_gather | solution.py:151
  73.4 174.2 %reduce-scatter.2.cloned.1.call-start = ((), (), s32[]{:S(2)}) async-start(), calls=%async_computation.12 | async-start | bytes 1769472 | tf_op jit(solution)/shard_map/reduce_scatter | solution.py:197
  84.9 95.9 %copy-start.9 = (f32[8192]{0:T(1024)S(1)}, f32[8192]{0:T(1024)}, u32[]{:S(2)}) copy-start(f32[8192]{0:T(1024)} %param.15) | copy-start | bytes 98308
  177.5 3.4 copy-start.3
  180.9 2.2 copy-start.2
  183.1 2.0 copy-start.1
  183.1 1.4 copy-start.8
  204.6 24.8 %all-to-all-start.3 = ((bf16[8,256,64]{1,2,0:T(8,128)(2,1)}), bf16[8,256,64]{1,2,0:T(8,128)(2,1)}, u32[]{:S(2)}, u32[]{:S(2)}) async-start(bf16[8,256,64]{1,2,0:T(8,128)(2,1)} %broadcast_in_dim.61), calls=%async_computation.4 | async-start | bytes 524288 | tf_op jit(solution)/shard_map/all_to_all | solution.py:33
  209.3 38.4 %slice-start = ((bf16[8192,192]{1,0:T(8,128)(2,1)}), bf16[8192,64]{1,0:T(8,128)(2,1)S(1)}, s32[]{:S(2)}) async-start(bf16[8192,192]{1,0:T(8,128)(2,1)} %all-gather.5.cloned.1.call-done), calls=%async_computation.13 | async-start | bytes 4194304 | tf_op jit(solution)/shard_map/split | solution.py:28
  232.6 44.8 %copy-start.17 = (s32[16]{0:T(128)S(1)}, s32[16]{0:T(128)}, u32[]{:S(2)}) copy-start(s32[16]{0:T(128)} %copy-done.16) | copy-start | bytes 196
  232.6 44.9 %copy-start.11 = (s32[16]{0:T(128)S(1)}, s32[16]{0:T(128)}, u32[]{:S(2)}) copy-start(s32[16]{0:T(128)} %copy-done.10) | copy-start | bytes 196
  250.0 14.7 %all-to-all-start.4 = ((bf16[16,6,1024]{2,1,0:T(8,128)(2,1)}), bf16[16,6,1024]{2,1,0:T(8,128)(2,1)S(1)}, u32[]{:S(2)}, u32[]{:S(2)}) async-start(bf16[16,6,1024]{2,1,0:T(8,128)(2,1)} %reshape.194), calls=%async_computation.5 | async-start | bytes 524288 | tf_op jit(solution)/shard_map/all_to_all | solution.py:213
  264.6 24.7 %all-to-all-start.7 = ((f32[64,1,1152]{2,1,0:T(1,128)}), f32[64,1,1152]{2,1,0:T(1,128)S(1)}, u32[]{:S(2)}, u32[]{:S(2)}) async-start(f32[64,1,1152]{2,1,0:T(1,128)} %bitcast.13), calls=%async_computation.8 | async-start | bytes 589824 | tf_op jit(solution)/shard_map/all_to_all | solution.py:57
  290.7 41.7 %all-to-all-start.5 = ((bf16[16,48,1024]{2,1,0:T(8,128)(2,1)}), bf16[16,48,1024]{2,1,0:T(8,128)(2,1)S(1)}, u32[]{:S(2)}, u32[]{:S(2)}) async-start(bf16[16,48,1024]{2,1,0:T(8,128)(2,1)} %broadcast_in_dim.62), calls=%async_computation.6 | async-start | bytes 3145728 | tf_op jit(solution)/shard_map/all_to_all | solution.py:33
  333.2 17.2 %all-to-all-start.8 = ((f32[64,1,1152]{2,1,0:T(1,128)}), f32[64,1,1152]{2,1,0:T(1,128)S(1)}, u32[]{:S(2)}, u32[]{:S(2)}) async-start(f32[64,1,1152]{2,1,0:T(1,128)} %broadcast_in_dim.64), calls=%async_computation.9 | async-start | bytes 589824 | tf_op jit(solution)/shard_map/all_to_all | solution.py:33
  350.5 1.8 copy-start.4
  352.3 34.9 %all-to-all-start.6 = ((bf16[4,320,1024]{2,1,0:T(8,128)(2,1)}), bf16[4,320,1024]{2,1,0:T(8,128)(2,1)S(1)}, u32[]{:S(2)}, u32[]{:S(2)}) async-start(bf16[4,320,1024]{2,1,0:T(8,128)(2,1)} %broadcast_in_dim.63), calls=%async_computation.7 | async-start | bytes 5242880 | tf_op jit(solution)/shard_map/all_to_all | solution.py:33
Sparse Core Ops, SparseCore 0:
  23.7 57.3 all-gather.4
  83.2 94.2 all-gather.2
  180.3 67.2 reduce-scatter.1
where the time goes:
time: 397 us; the launch traced here: 395 us
  waiting for transfers between devices  257 us (65%)
  starting transfers between devices  53.8 us (14%)
  local copies, waits for them, and re-layouts  21.2 us (5%)
  matrix products  18 us (5%)
  blocking collectives  16.1 us (4%)
  other arithmetic  14.8 us (4%)
  between operations  14.1 us (4%)
    all_gather x1, waiting for transfers between devices, shards(): gathered = lax.all_gather(inputs, 'tp', axis=1, tiled=True)  92.6 us
    all_to_all x4, waiting for transfers between devices, copy_for_each(): return lax.all_to_all(copies, axis, split_axis=0, concat_axis=0, tiled=True)  83.7 us
    all_to_all x1, waiting for transfers between devices, sent_and_summed(): blocks = lax.all_to_all(in_blocks(x, dim, length), axis, 0, 0, tiled=True)  33.4 us
    all_to_all x4, starting transfers between devices, copy_for_each(): return lax.all_to_all(copies, axis, split_axis=0, concat_axis=0, tiled=True)  20 us
    all_to_all x1, blocking collectives, copy_for_each(): return lax.all_to_all(copies, axis, split_axis=0, concat_axis=0, tiled=True)  16.1 us
    reduce_scatter x1, waiting for transfers between devices, shards(): lax.psum_scatter(spread_rows.astype(jnp.bfloat16), 'tp', scatter_dimensio...  15 us
    all_to_all x1, starting transfers between devices, sum_at_owner(): lax.all_to_all(blocks, axis, split_axis=0, concat_axis=0, tiled=True)  12.8 us
    all_to_all x1, waiting for transfers between devices, sum_at_owner(): lax.all_to_all(blocks, axis, split_axis=0, concat_axis=0, tiled=True)  11.3 us
  transfers between devices with their start and end apart: 11, of which 11 were waited for; matrix products, arithmetic and copies ran while one was open for 10% of the time, Pallas kernels for 0%

commit v1 on v0

--- a/solution.py
+++ b/solution.py
@@ -148,7 +148,9 @@
         jnp.bfloat16
     )
     inputs = jnp.where(is_audio[:, None], audio_part, text_token_embedding)
-    gathered = lax.all_gather(inputs, "tp", axis=1, tiled=True)
+    gathered = jnp.concatenate(
+        lax.all_to_all(jnp.stack([inputs] * lax.axis_size("tp")), "tp", 0, 0), axis=1
+    )
     widened = gathered.astype(jnp.float32)
     mean_sq = jnp.mean(widened * widened, axis=1)
     inv_rms = lax.rsqrt(mean_sq + norm_eps)

time: 397 us -> 496 us (1.25)
  waiting for transfers between devices: 257 us -> 350 us
  starting transfers between devices: 53.8 us -> 59.3 us
    all_to_all x0 -> x1, waiting for transfers between devices: none -> 148 us  [shards(): lax.all_to_all(jnp.stack([inputs] * lax.axis_size('tp')), 'tp', 0, 0)]
    all_gather x1 -> x0, waiting for transfers between devices: 92.6 us -> none  [shards(): gathered = lax.all_gather(inputs, 'tp', axis=1, tiled=True)]
    all_gather x1, waiting for transfers between devices: 7.23 us -> 58.6 us  [side_by_side(): lax.all_gather(both, axis, axis=dim, tiled=True)]
    reduce_scatter x1, waiting for transfers between devices: 15 us -> 0.02 us  [shards(): lax.psum_scatter(spread_rows.astype(jnp.bfloat16), 'tp', scatter_dimensio...]
    all_to_all x0 -> x1, starting transfers between devices: none -> 12.5 us  [shards(): lax.all_to_all(jnp.stack([inputs] * lax.axis_size('tp')), 'tp', 0, 0)]
  transfers between devices with their start and end apart: 11 -> 11, of which waited for: 11 -> 10; matrix products, arithmetic and copies ran while one was open for 10% -> 7% of each run, Pallas kernels for 0% -> 0%
where the time goes in v1:
time: 496 us; the launch traced here: 495 us
  waiting for transfers between devices  350 us (71%)
  starting transfers between devices  59.3 us (12%)
  local copies, waits for them, and re-layouts  23.2 us (5%)
  matrix products  17.4 us (4%)
  other arithmetic  15.5 us (3%)
  blocking collectives  14.8 us (3%)
  between operations  14.5 us (3%)
    all_to_all x1, waiting for transfers between devices, shards(): lax.all_to_all(jnp.stack([inputs] * lax.axis_size('tp')), 'tp', 0, 0)  148 us
    all_to_all x4, waiting for transfers between devices, copy_for_each(): return lax.all_to_all(copies, axis, split_axis=0, concat_axis=0, tiled=True)  83.2 us
    all_gather x1, waiting for transfers between devices, side_by_side(): lax.all_gather(both, axis, axis=dim, tiled=True)  58.6 us
    all_to_all x1, waiting for transfers between devices, sent_and_summed(): blocks = lax.all_to_all(in_blocks(x, dim, length), axis, 0, 0, tiled=True)  35 us
    all_to_all x4, starting transfers between devices, copy_for_each(): return lax.all_to_all(copies, axis, split_axis=0, concat_axis=0, tiled=True)  19.9 us
    all_to_all x1, blocking collectives, copy_for_each(): return lax.all_to_all(copies, axis, split_axis=0, concat_axis=0, tiled=True)  14.8 us
    all_to_all x1, starting transfers between devices, shards(): lax.all_to_all(jnp.stack([inputs] * lax.axis_size('tp')), 'tp', 0, 0)  12.5 us
    all_to_all x1, waiting for transfers between devices, sum_at_owner(): lax.all_to_all(blocks, axis, split_axis=0, concat_axis=0, tiled=True)  10.1 us
  transfers between devices with their start and end apart: 11, of which 10 were waited for; matrix products, arithmetic and copies ran while one was open for 7% of the time, Pallas kernels for 0%

profile of v1, /device:TPU:64, one launch (start us, length us, event | category | flops | bytes accessed | tf_op | source)
XLA Modules:
  0.0 494.6 jit_solution(1897537474639367126)
XLA Ops:
  7.2 1.1 copy-done
  8.3 3.2 convolution_convert_fusion.1
  11.5 8.6 %all-to-all-start = ((bf16[16,48,1024]{2,1,0:T(8,128)(2,1)}), bf16[16,48,1024]{2,1,0:T(8,128)(2,1)S(1)}, u32[]{:S(2)}, u32[]{:S(2)}) async-start(bf16[16,48,1024]{2,1,0:T(8,128)(2,1)} %bitcast.59), calls=%async_computation | async-start | bytes 3145728 | tf_op jit(solution)/shard_map/all_to_all | solution.py:18
  21.5 35.0 %all-to-all-done = bf16[16,48,1024]{2,1,0:T(8,128)(2,1)S(1)} async-done(((bf16[16,48,1024]{2,1,0:T(8,128)(2,1)}), bf16[16,48,1024]{2,1,0:T(8,128)(2,1)S(1)}, u32[]{:S(2)}, u32[]{:S(2)}) %all-to-all-start) | async-done | bytes 1572896 | tf_op jit(solution)/shard_map/all_to_all | solution.py:18
  57.0 0.8 reshape.199
  57.8 5.1 %all-to-all-start.1 = ((bf16[16,6,1024]{2,1,0:T(8,128)(2,1)}), bf16[16,6,1024]{2,1,0:T(8,128)(2,1)S(1)}, u32[]{:S(2)}, u32[]{:S(2)}) async-start(bf16[16,6,1024]{2,1,0:T(8,128)(2,1)} %reshape.199), calls=%async_computation.1 | async-start | bytes 524288 | tf_op jit(solution)/shard_map/all_to_all | solution.py:144
  63.1 7.8 %all-to-all-done.1 = bf16[16,6,1024]{2,1,0:T(8,128)(2,1)S(1)} async-done(((bf16[16,6,1024]{2,1,0:T(8,128)(2,1)}), bf16[16,6,1024]{2,1,0:T(8,128)(2,1)S(1)}, u32[]{:S(2)}, u32[]{:S(2)}) %all-to-all-start.1) | async-done | bytes 196640 | tf_op jit(solution)/shard_map/all_to_all | solution.py:144
  70.9 1.4 fusion.7
  72.6 2.2 stack.6
  74.8 12.5 %all-to-all-start.2 = ((bf16[8,256,1024]{1,2,0:T(8,128)(2,1)}), bf16[8,256,1024]{1,2,0:T(8,128)(2,1)}, u32[]{:S(2)}, u32[]{:S(2)}) async-start(bf16[8,256,1024]{1,2,0:T(8,128)(2,1)} %stack.6), calls=%async_computation.2 | async-start | bytes 8388608 | tf_op jit(solution)/shard_map/all_to_all | solution.py:152
  87.7 1.2 pad_maximum_fusion
  89.2 58.6 %all-gather.2.cloned.1.call-done = bf16[8192,192]{1,0:T(8,128)(2,1)} async-done(((bf16[2048,192]{1,0:T(8,128)(2,1)}), bf16[8192,192]{1,0:T(8,128)(2,1)}) %all-gather.2.cloned.1.call-update) | async-done | bytes 3145744 | tf_op jit(solution)/shard_map/all_gather | solution.py:28
  147.8 3.8 convolution_convert_fusion
  151.6 148.3 %all-to-all-done.2 = bf16[8,256,1024]{1,2,0:T(8,128)(2,1)} async-done(((bf16[8,256,1024]{1,2,0:T(8,128)(2,1)}), bf16[8,256,1024]{1,2,0:T(8,128)(2,1)}, u32[]{:S(2)}, u32[]{:S(2)}) %all-to-all-start.2) | async-done | bytes 4194336 | tf_op jit(solution)/shard_map/all_to_all | solution.py:152
  299.9 3.3 multiply_reduce_fusion
  303.3 3.0 fusion.1
  306.7 1.0 fusion.70
  307.9 0.8 copy-done.1
  308.7 1.6 multiply_reduce_fusion.1
  311.5 14.8 %all_to_all.56 = bf16[8,2,128]{2,1,0:T(2,128)(2,1)S(1)} all-to-all(bf16[8,2,128]{2,1,0:T(2,128)(2,1)S(1)} %reshape.210), channel_id=1, replica_groups=mesh['grp'=16,'fsdp'=4,'tp'=8] {'tp'}, dimensions={0} | all-to-all | bytes 8192 | tf_op jit(solution)/shard_map/all_to_all | solution.py:33
  327.1 3.4 all-to-all-start.4
  331.1 0.8 reshape.205
  331.9 0.8 fusion.14
  333.5 18.3 %all-to-all-done.4 = bf16[8,256,64]{1,2,0:T(8,128)(2,1)S(1)} async-done(((bf16[8,256,64]{1,2,0:T(8,128)(2,1)}), bf16[8,256,64]{1,2,0:T(8,128)(2,1)S(1)}, u32[]{:S(2)}, u32[]{:S(2)}) %all-to-all-start.4) | async-done | bytes 262176 | tf_op jit(solution)/shard_map/all_to_all | solution.py:33
  352.4 1.3 fusion.15
  353.9 1.5 fusion.10
  355.4 0.8 reshape.200
  356.2 4.2 all-to-all-start.5
  360.4 1.5 pad_maximum_fusion.1
  361.9 6.8 %all-to-all-done.5 = bf16[16,6,1024]{2,1,0:T(8,128)(2,1)S(1)} async-done(((bf16[16,6,1024]{2,1,0:T(8,128)(2,1)}), bf16[16,6,1024]{2,1,0:T(8,128)(2,1)S(1)}, u32[]{:S(2)}, u32[]{:S(2)}) %all-to-all-start.5) | async-done | bytes 196640 | tf_op jit(solution)/shard_map/all_to_all | solution.py:215
  368.7 8.9 %all-to-all-start.8 = ((f32[64,1,1152]{2,1,0:T(1,128)}), f32[64,1,1152]{2,1,0:T(1,128)S(1)}, u32[]{:S(2)}, u32[]{:S(2)}) async-start(f32[64,1,1152]{2,1,0:T(1,128)} %bitcast.15), calls=%async_computation.9 | async-start | bytes 589824 | tf_op jit(solution)/shard_map/all_to_all | solution.py:57
  378.2 10.1 %all-to-all-done.8 = f32[64,1,1152]{2,1,0:T(1,128)S(1)} async-done(((f32[64,1,1152]{2,1,0:T(1,128)}), f32[64,1,1152]{2,1,0:T(1,128)S(1)}, u32[]{:S(2)}, u32[]{:S(2)}) %all-to-all-start.8) | async-done | bytes 294944 | tf_op jit(solution)/shard_map/all_to_all | solution.py:57
  388.4 1.4 broadcast_in_dim.62
  389.7 5.7 %all-to-all-start.6 = ((bf16[16,48,1024]{2,1,0:T(8,128)(2,1)}), bf16[16,48,1024]{2,1,0:T(8,128)(2,1)S(1)}, u32[]{:S(2)}, u32[]{:S(2)}) async-start(bf16[16,48,1024]{2,1,0:T(8,128)(2,1)} %broadcast_in_dim.62), calls=%async_computation.7 | async-start | bytes 3145728 | tf_op jit(solution)/shard_map/all_to_all | solution.py:33
  395.6 35.4 %all-to-all-done.6 = bf16[16,48,1024]{2,1,0:T(8,128)(2,1)S(1)} async-done(((bf16[16,48,1024]{2,1,0:T(8,128)(2,1)}), bf16[16,48,1024]{2,1,0:T(8,128)(2,1)S(1)}, u32[]{:S(2)}, u32[]{:S(2)}) %all-to-all-start.6) | async-done | bytes 1572896 | tf_op jit(solution)/shard_map/all_to_all | solution.py:33
  431.0 0.9 broadcast_in_dim.64
  431.8 7.0 %all-to-all-start.9 = ((f32[64,1,1152]{2,1,0:T(1,128)}), f32[64,1,1152]{2,1,0:T(1,128)S(1)}, u32[]{:S(2)}, u32[]{:S(2)}) async-start(f32[64,1,1152]{2,1,0:T(1,128)} %broadcast_in_dim.64), calls=%async_computation.10 | async-start | bytes 589824 | tf_op jit(solution)/shard_map/all_to_all | solution.py:33
  438.9 1.7 fusion.6
  440.6 8.8 %all-to-all-done.9 = f32[64,1,1152]{2,1,0:T(1,128)S(1)} async-done(((f32[64,1,1152]{2,1,0:T(1,128)}), f32[64,1,1152]{2,1,0:T(1,128)S(1)}, u32[]{:S(2)}, u32[]{:S(2)}) %all-to-all-start.9) | async-done | bytes 294944 | tf_op jit(solution)/shard_map/all_to_all | solution.py:33
  449.4 1.9 broadcast_in_dim.63
  451.3 3.8 all-to-all-start.7
  456.0 2.4 reduce.7
  458.4 1.9 slice.20
  460.3 1.9 slice.24
  462.2 1.9 copy.103
  464.1 1.4 slice.25
  465.5 20.7 %all-to-all-done.7 = bf16[4,320,1024]{2,1,0:T(8,128)(2,1)S(1)} async-done(((bf16[4,320,1024]{2,1,0:T(8,128)(2,1)}), bf16[4,320,1024]{2,1,0:T(8,128)(2,1)S(1)}, u32[]{:S(2)}, u32[]{:S(2)}) %all-to-all-start.7) | async-done | bytes 2621472 | tf_op jit(solution)/shard_map/all_to_all | solution.py:33
  486.3 1.5 convert_reduce_fusion
  (102 shorter events, 9.5 us)
Async XLA Ops:
  7.2 1.1 copy-start
  7.2 12.9 %copy-start.15 = (s32[1,16,16]{2,1,0:T(8,128)S(1)}, s32[1,16,16]{2,1,0:T(8,128)}, u32[]{:S(2)}) copy-start(s32[1,16,16]{2,1,0:T(8,128)} %param.19) | copy-start | bytes 3076
  7.2 12.9 %copy-start.16 = (s32[1,16,16]{2,1,0:T(8,128)S(1)}, s32[1,16,16]{2,1,0:T(8,128)}, u32[]{:S(2)}) copy-start(s32[1,16,16]{2,1,0:T(8,128)} %param.20) | copy-start | bytes 3076
  11.5 45.0 %all-to-all-start = ((bf16[16,48,1024]{2,1,0:T(8,128)(2,1)}), bf16[16,48,1024]{2,1,0:T(8,128)(2,1)S(1)}, u32[]{:S(2)}, u32[]{:S(2)}) async-start(bf16[16,48,1024]{2,1,0:T(8,128)(2,1)} %bitcast.59), calls=%async_computation | async-start | bytes 3145728 | tf_op jit(solution)/shard_map/all_to_all | solution.py:18
  20.2 1.2 copy-start.13
  20.4 0.5 copy-start.19
  21.4 311.3 %copy-start.17 = (s32[96]{0:T(128)}, s32[96]{0:T(128)S(1)}, u32[]{:S(2)}) copy-start(s32[96]{0:T(128)S(1)} %get-tuple-element.41) | copy-start | bytes 1156
  21.4 311.3 %copy-start.18 = (pred[96]{0:T(512)(128)(4,1)}, pred[96]{0:T(512)(128)(4,1)S(1)}, u32[]{:S(2)}) copy-start(pred[96]{0:T(512)(128)(4,1)S(1)} %get-tuple-element.39) | copy-start | bytes 292
  57.8 13.1 %all-to-all-start.1 = ((bf16[16,6,1024]{2,1,0:T(8,128)(2,1)}), bf16[16,6,1024]{2,1,0:T(8,128)(2,1)S(1)}, u32[]{:S(2)}, u32[]{:S(2)}) async-start(bf16[16,6,1024]{2,1,0:T(8,128)(2,1)} %reshape.199), calls=%async_computation.1 | async-start | bytes 524288 | tf_op jit(solution)/shard_map/all_to_all | solution.py:144
  74.8 12.6 %copy-start.8 = (bf16[2048,64]{0,1:T(8,128)(2,1)S(1)}, bf16[2048,64]{0,1:T(8,128)(2,1)}, u32[]{:S(2)}) copy-start(bf16[2048,64]{0,1:T(8,128)(2,1)} %param.17) | copy-start | bytes 786436
  74.8 12.9 %copy-start.6 = (bf16[2048,128]{1,0:T(8,128)(2,1)S(1)}, bf16[2048,128]{1,0:T(8,128)(2,1)}, u32[]{:S(2)}) copy-start(bf16[2048,128]{1,0:T(8,128)(2,1)} %param.16) | copy-start | bytes 1572868
  74.8 225.1 %all-to-all-start.2 = ((bf16[8,256,1024]{1,2,0:T(8,128)(2,1)}), bf16[8,256,1024]{1,2,0:T(8,128)(2,1)}, u32[]{:S(2)}, u32[]{:S(2)}) async-start(bf16[8,256,1024]{1,2,0:T(8,128)(2,1)} %stack.6), calls=%async_computation.2 | async-start | bytes 8388608 | tf_op jit(solution)/shard_map/all_to_all | solution.py:152
  87.3 1.6 copy-start.10
  87.3 1.7 copy-start.21
  87.3 1.7 copy-start.22
  87.3 60.5 %all-gather.2.cloned.1.call-start = ((), (), s32[]{:S(2)}) async-start(), calls=%async_computation.11 | async-start | bytes 5242880 | tf_op jit(solution)/shard_map/all_gather | solution.py:28
  88.9 265.0 %reduce-scatter.2.cloned.1.call-start = ((), (), s32[]{:S(2)}) async-start(), calls=%async_computation.12 | async-start | bytes 1769472 | tf_op jit(solution)/shard_map/reduce_scatter | solution.py:199
  151.6 151.7 %copy-start.12 = (f32[8192]{0:T(1024)S(1)}, f32[8192]{0:T(1024)}, u32[]{:S(2)}) copy-start(f32[8192]{0:T(1024)} %param.15) | copy-start | bytes 98308
  303.3 3.5 copy-start.2
  306.7 2.0 copy-start.1
  306.7 1.0 copy-start.11
  307.7 24.2 %copy-start.4 = (f32[256,64]{0,1:T(8,128)}, f32[256,64]{0,1:T(8,128)S(1)}, u32[]{:S(2)}) copy-start(f32[256,64]{0,1:T(8,128)S(1)} %fusion.70) | copy-start | bytes 196612
  327.1 24.7 %all-to-all-start.4 = ((bf16[8,256,64]{1,2,0:T(8,128)(2,1)}), bf16[8,256,64]{1,2,0:T(8,128)(2,1)S(1)}, u32[]{:S(2)}, u32[]{:S(2)}) async-start(bf16[8,256,64]{1,2,0:T(8,128)(2,1)} %broadcast_in_dim.61), calls=%async_computation.5 | async-start | bytes 524288 | tf_op jit(solution)/shard_map/all_to_all | solution.py:33
  331.1 22.8 %slice-start = ((bf16[8192,192]{1,0:T(8,128)(2,1)}), bf16[8192,64]{1,0:T(8,128)(2,1)S(1)}, s32[]{:S(2)}) async-start(bf16[8192,192]{1,0:T(8,128)(2,1)} %all-gather.2.cloned.1.call-done), calls=%async_computation.13 | async-start | bytes 4194304 | tf_op jit(solution)/shard_map/split | solution.py:28
  351.8 0.6 copy-start.7
  353.9 23.8 %copy-start.20 = (s32[16]{0:T(128)S(1)}, s32[16]{0:T(128)}, u32[]{:S(2)}) copy-start(s32[16]{0:T(128)} %copy-done.19) | copy-start | bytes 196
  353.9 23.9 %copy-start.14 = (s32[16]{0:T(128)S(1)}, s32[16]{0:T(128)}, u32[]{:S(2)}) copy-start(s32[16]{0:T(128)} %copy-done.13) | copy-start | bytes 196
  356.2 12.5 %all-to-all-start.5 = ((bf16[16,6,1024]{2,1,0:T(8,128)(2,1)}), bf16[16,6,1024]{2,1,0:T(8,128)(2,1)S(1)}, u32[]{:S(2)}, u32[]{:S(2)}) async-start(bf16[16,6,1024]{2,1,0:T(8,128)(2,1)} %reshape.200), calls=%async_computation.6 | async-start | bytes 524288 | tf_op jit(solution)/shard_map/all_to_all | solution.py:215
  368.7 19.6 %all-to-all-start.8 = ((f32[64,1,1152]{2,1,0:T(1,128)}), f32[64,1,1152]{2,1,0:T(1,128)S(1)}, u32[]{:S(2)}, u32[]{:S(2)}) async-start(f32[64,1,1152]{2,1,0:T(1,128)} %bitcast.15), calls=%async_computation.9 | async-start | bytes 589824 | tf_op jit(solution)/shard_map/all_to_all | solution.py:57
  389.7 41.2 %all-to-all-start.6 = ((bf16[16,48,1024]{2,1,0:T(8,128)(2,1)}), bf16[16,48,1024]{2,1,0:T(8,128)(2,1)S(1)}, u32[]{:S(2)}, u32[]{:S(2)}) async-start(bf16[16,48,1024]{2,1,0:T(8,128)(2,1)} %broadcast_in_dim.62), calls=%async_computation.7 | async-start | bytes 3145728 | tf_op jit(solution)/shard_map/all_to_all | solution.py:33
  431.8 17.6 %all-to-all-start.9 = ((f32[64,1,1152]{2,1,0:T(1,128)}), f32[64,1,1152]{2,1,0:T(1,128)S(1)}, u32[]{:S(2)}, u32[]{:S(2)}) async-start(f32[64,1,1152]{2,1,0:T(1,128)} %broadcast_in_dim.64), calls=%async_computation.10 | async-start | bytes 589824 | tf_op jit(solution)/shard_map/all_to_all | solution.py:33
  449.4 1.9 copy-start.3
  451.3 3.8 copy-start.5
  451.3 3.8 copy-start.9
  451.3 35.0 %all-to-all-start.7 = ((bf16[4,320,1024]{2,1,0:T(8,128)(2,1)}), bf16[4,320,1024]{2,1,0:T(8,128)(2,1)S(1)}, u32[]{:S(2)}, u32[]{:S(2)}) async-start(bf16[4,320,1024]{2,1,0:T(8,128)(2,1)} %broadcast_in_dim.63), calls=%async_computation.8 | async-start | bytes 5242880 | tf_op jit(solution)/shard_map/all_to_all | solution.py:33
Sparse Core Ops, SparseCore 0:
  90.8 56.9 all-gather.1
  151.7 125.5 reduce-scatter.1
